TPU v7x, 32 devices: a whole 2x2x4 slice. The times are simulated.
32 devices in a mesh: dp: 8 (over y, x, core), tensor: 4 (over z).
Axes of the slice: x: 2, y: 2, z: 4, core: 2. Of those that a mesh axis runs over, the one named last changes fastest.
Arguments:
- queries: bfloat16 [2048, 8192], P('dp', 'tensor'), may hold values from -5 to 5
- keys_values: bfloat16 [2, 2048, 1024], P(None, 'dp', 'tensor'), may hold values from -5 to 5
- grad_out: bfloat16 [2048, 8192], P(('dp', 'tensor')), may hold values from -6 to 6
- piece_lengths: int32 [12], replicated, may hold values from 64 to 448, as said below
Outputs:
- grad_queries: bfloat16 [2048, 8192], P(('dp', 'tensor'))
- grad_keys_values: bfloat16 [2, 2048, 1024], P(None, 'dp', 'tensor')
Inputs may be any that keep to these rules, and one draw needn't show every extreme that they name: `piece_lengths`: entry 3p (p < 4) is the length of prompt p, entries 3p + 1 and 3p + 2 the lengths of its chosen and rejected responses; the entries sum to 2048; a prompt with its two responses holds at most 36 * (32) rows.
All inputs are finite; a program needn't handle non-finite values.
Results may differ from a plain program's by a relative error of at most 0.028.
Values may be sent and summed in bfloat16 or wider, within the bound.
A program may use at most 128 MiB of HBM per device.

v0:
```python
import math

import jax
import jax.numpy as jnp
from jax import lax
from jax.sharding import PartitionSpec as P

HEAD_DIM = 128


def piece_index(row_ids, piece_ends):
    return jnp.sum((row_ids[:, None] >= piece_ends[None, :]).astype(jnp.int32), axis=1)


def visible(query_ids, query_piece, key_ids, key_piece):
    same_piece = key_piece[None, :] == query_piece[:, None]
    own_prompt = key_piece[None, :] == 3 * (query_piece[:, None] // 3)
    inside = (key_ids >= 0)[None, :]
    return (key_ids[None, :] <= query_ids[:, None]) & (same_piece | own_prompt) & inside


def body(queries, keys_values, grad_out, piece_lengths):
    row_count = queries.shape[0]
    width = queries.shape[1]
    head_dim = HEAD_DIM
    kv_width = keys_values.shape[2]
    kv_dev = kv_width // head_dim
    group_size = width // head_dim // kv_dev
    inv_root = 1.0 / math.sqrt(head_dim)
    grad_local = lax.all_to_all(grad_out, "tensor", split_axis=1, concat_axis=0, tiled=True)
    piece_ends = jnp.cumsum(piece_lengths)
    own_start = lax.axis_index("dp") * row_count
    query_ids = own_start + jnp.arange(row_count, dtype=jnp.int32)
    query_piece = piece_index(query_ids, piece_ends)
    q_four = queries.reshape(row_count, kv_dev, group_size, head_dim)
    g_four = grad_local.reshape(row_count, kv_dev, group_size, head_dim)

    def mask_of(key_count):
        key_ids = jnp.arange(key_count, dtype=jnp.int32)
        return visible(query_ids, query_piece, key_ids, piece_index(key_ids, piece_ends))

    def logits_of(kv_block):
        key_count = kv_block.shape[1]
        keys_three = kv_block[0].reshape(key_count, kv_dev, head_dim)
        logits = jnp.einsum(
            "rkgd,nkd->kgrn", q_four, keys_three, preferred_element_type=jnp.float32
        )
        return logits * inv_root

    start_state = (
        jnp.full((kv_dev, group_size, row_count), -1e30, jnp.float32),
        jnp.zeros((kv_dev, group_size, row_count), jnp.float32),
        jnp.zeros((kv_dev, group_size, row_count, head_dim), jnp.float32),
    )

    def backward_parts(kv_block, allowed):
        key_count = kv_block.shape[1]
        logits = logits_of(kv_block)
        attend = jnp.where(
            allowed[None, None], jnp.exp(logits - log_total[..., None]), jnp.float32(0.0)
        )
        values_three = kv_block[1].reshape(key_count, kv_dev, head_dim)
        keys_three = kv_block[0].reshape(key_count, kv_dev, head_dim)
        pushed = jnp.einsum(
            "rkgd,nkd->kgrn", g_four, values_three, preferred_element_type=jnp.float32
        )
        slopes = (attend * (pushed - row_delta[..., None])).astype(jnp.bfloat16)
        return (attend.astype(jnp.bfloat16), slopes, keys_three)

    def query_term(slopes, keys_three):
        return (
            jnp.einsum("kgrn,nkd->rkgd", slopes, keys_three, preferred_element_type=jnp.float32)
            * inv_root
        )

    def key_term(attend_low, slopes):
        key_count = slopes.shape[3]
        key_part = (
            jnp.einsum("kgrn,rkgd->nkd", slopes, q_four, preferred_element_type=jnp.float32)
            * inv_root
        )
        value_part = jnp.einsum(
            "kgrn,rkgd->nkd", attend_low, g_four, preferred_element_type=jnp.float32
        )
        return jnp.stack(
            [key_part.reshape(key_count, kv_width), value_part.reshape(key_count, kv_width)]
        )

    kv_block = lax.all_gather(keys_values, "dp", axis=1, tiled=True)
    key_count = kv_block.shape[1]
    allowed = mask_of(key_count)

    def compute(carry_state):
        row_top, row_total, weighted = carry_state
        logits = logits_of(kv_block)
        masked = jnp.where(allowed[None, None], logits, jnp.float32(-1e30))
        new_top = jnp.maximum(row_top, jnp.max(masked, axis=-1))
        weights = jnp.where(
            allowed[None, None], jnp.exp(logits - new_top[..., None]), jnp.float32(0.0)
        )
        values_three = kv_block[1].reshape(key_count, kv_dev, head_dim)
        added = jnp.einsum(
            "kgrn,nkd->kgrd",
            weights.astype(jnp.bfloat16),
            values_three,
            preferred_element_type=jnp.float32,
        )
        return (new_top, jnp.sum(weights, axis=-1), added)

    row_top, row_total, weighted = compute(start_state)
    log_total = row_top + jnp.log(row_total)
    outputs = (weighted / row_total[..., None]).astype(jnp.bfloat16)
    row_delta = jnp.sum(
        g_four.astype(jnp.float32).transpose(1, 2, 0, 3) * outputs.astype(jnp.float32), axis=-1
    )
    query_start = jnp.zeros((row_count, kv_dev, group_size, head_dim), jnp.float32)
    key_start = jnp.zeros((2, row_count * lax.axis_size("dp"), kv_width), jnp.float32)
    backward_kv_block = lax.all_gather(keys_values, "dp", axis=1, tiled=True)
    backward_key_count = backward_kv_block.shape[1]
    backward_allowed = mask_of(backward_key_count)

    def compute(carry_state):
        attend_low, slopes, keys_three = backward_parts(backward_kv_block, backward_allowed)
        query_grad = query_term(slopes, keys_three)
        key_grad = key_term(attend_low, slopes)
        return (query_grad, key_grad)

    query_grad, key_grad = compute((query_start, key_start))
    key_own = lax.psum_scatter(key_grad.astype(jnp.bfloat16), "dp", scatter_dimension=1, tiled=True)
    query_low = query_grad.reshape(row_count, width).astype(jnp.bfloat16)
    grad_queries = lax.all_to_all(query_low, "tensor", split_axis=0, concat_axis=1, tiled=True)
    return (grad_queries, key_own)


def solution(mesh):
    return jax.shard_map(
        body,
        mesh=mesh,
        in_specs=(P("dp", "tensor"), P(None, "dp", "tensor"), P(("dp", "tensor"), None), P()),
        out_specs=(P(("dp", "tensor"), None), P(None, "dp", "tensor")),
        check_vma=False,
    )
```

profile of v0, /device:TPU:0, one launch (start us, length us, event | category | flops | bytes accessed | tf_op | source)
XLA Modules:
  0.0 187.9 jit_solution(1538652631539022592)
XLA Ops:
  7.2 0.0 all-gather.2.cloned.1.call-start
  7.2 1.8 copy.52
  9.0 0.0 all-gather.2.cloned.1.call-update
  9.0 2.3 %copy.91 = bf16[8,4,8,2048]{3,2,0,1:T(8,128)(2,1)} copy(bf16[8,4,8,2048]{3,2,1,0:T(8,128)(2,1)} %bitcast.111) | data formatting | bytes 2097152 | tf_op jit(solution)/shard_map/all_to_all | solution.py:30
  11.3 6.3 %all-to-all-start = ((bf16[64,4,2048]{2,0,1:T(8,128)(2,1)}), bf16[64,4,2048]{2,0,1:T(8,128)(2,1)S(1)}, u32[]{:S(2)}, u32[]{:S(2)}) async-start(bf16[64,4,2048]{2,0,1:T(8,128)(2,1)} %bitcast.102), calls=%async_computation | async-start | bytes 2097152 | tf_op jit(solution)/shard_map/all_to_all | solution.py:30
  17.6 0.0 reduce-scatter.2.cloned.1.call-start
  17.7 1.5 copy.86
  19.1 0.8 reduce-window.8
  20.0 0.1 convert_reduce_fusion.1
  20.1 0.1 convert_reduce_fusion
  20.2 0.7 fusion.25
  20.9 22.5 %all-to-all-done = bf16[64,4,2048]{2,0,1:T(8,128)(2,1)S(1)} async-done(((bf16[64,4,2048]{2,0,1:T(8,128)(2,1)}), bf16[64,4,2048]{2,0,1:T(8,128)(2,1)S(1)}, u32[]{:S(2)}, u32[]{:S(2)}) %all-to-all-start) | async-done | bytes 1048608 | tf_op jit(solution)/shard_map/all_to_all | solution.py:30
  43.4 1.2 copy.89
  44.6 2.4 %copy.58 = bf16[256,2,8,128]{0,3,2,1:T(8,128)(2,1)} copy(bf16[256,2,8,128]{3,2,1,0:T(8,128)(2,1)} %bitcast.109) | data formatting | bytes 2097152 | tf_op jit(solution)/shard_map/reshape | solution.py:36
  47.0 0.0 all-gather.2.cloned.1.call-done
  47.0 1.7 fusion.36
  48.7 0.0 copy-start.1
  48.7 0.0 copy-start
  48.7 13.5 %fusion.2 = (f32[2,8,256]{2,1,0:T(8,128)S(1)}, f32[2,2048,256,8]{2,1,3,0:T(8,128)}) fusion(pred[256,2048]{0,1:T(8,128)(4,1)S(1)} %fusion.25, bf16[2048,2,128,1]{0,2,3,1:T(8,128)(2,1)S(1)} %bitcast.105, bf16[256,2,8,128]{0,3,2,1:T(8,128)(2,1)S(1)} %bitcast.103), kind=kOutput, calls=%fused_computation.6 | convolution fusion | flops 2172645376 | bytes 36192256 | tf_op jit(solution)/shard_map/rkgd,nkd->kgrn/dot_general | solution.py:45
  62.2 14.4 %fusion.9 = f32[2,8,256]{2,1,0:T(8,128)S(1)} fusion(f32[2,2048,256,8]{2,1,3,0:T(8,128)} %get-tuple-element.5, f32[2,8,256]{2,1,0:T(8,128)S(1)} %broadcast_maximum_fusion, pred[256,2048]{0,1:T(8,128)(4,1)S(1)} %fusion.25), kind=kLoop, calls=%fused_computation.13 | loop fusion | flops 33550336 | bytes 34111488 | tf_op jit(solution)/shard_map/reduce_sum | solution.py:108
  76.6 0.0 copy-done.1
  76.6 0.0 copy-done
  76.6 13.9 %fusion.24 = f32[2,8,256]{2,1,0:T(8,128)S(1)} fusion(bf16[256,2,8,128]{0,3,2,1:T(8,128)(2,1)S(1)} %copy-done, f32[2,8,256]{2,1,0:T(8,128)S(1)} %fusion.9, bf16[2048,2,128,1]{0,2,3,1:T(8,128)(2,1)S(1)} %bitcast.114, f32[2,2048,256,8]{2,1,3,0:T(8,128)} %get-tuple-element.5, f32[2,8,256]{2,1,0:T(8,128)S(1)} %broadcast_maximum_fusion, ...), kind=kOutput, calls=%fused_computation.25 | convolution fusion | flops 2184179712 | bytes 36225024 | tf_op jit(solution)/shard_map/kgrn,nkd->kgrd/dot_general | solution.py:102
  90.5 15.4 %fusion.21 = bf16[2,2048,128]{1,2,0:T(8,128)(2,1)} fusion(bf16[256,2,8,128]{0,3,2,1:T(8,128)(2,1)} %copy.58, f32[2,2048,256,8]{2,1,3,0:T(8,128)} %get-tuple-element.5, f32[2,8,256]{2,1,0:T(8,128)S(1)} %log_add_fusion, pred[256,2048]{0,1:T(8,128)(4,1)S(1)} %fusion.25), kind=kOutput, calls=%fused_computation.22 | convolution fusion | flops 2181562368 | bytes 36192256 | tf_op jit(solution)/shard_map/kgrn,rkgd->nkd/dot_general | solution.py:82
  105.9 19.8 %fusion.1 = bf16[2,8,256,2048]{2,3,1,0:T(8,128)(2,1)} fusion(f32[2,2048,256,8]{2,1,3,0:T(8,128)} %get-tuple-element.5, f32[2,8,256]{2,1,0:T(8,128)S(1)} %fusion.24, f32[2,8,256]{2,1,0:T(8,128)S(1)} %log_add_fusion, pred[256,2048]{0,1:T(8,128)(4,1)S(1)} %fusion.25, bf16[2048,2,128,1]{0,2,3,1:T(8,128)(2,1)} %bitcast.115, bf16[256,2,8,128]{0,3,2,1:T(8,128)(2,1)} %copy.58), kind=kOutput, calls=%fused_computation.2 | convolution fusion | flops 2197815296 | bytes 52985856 | tf_op jit(solution)/shard_map/rkgd,nkd->kgrn/dot_general | solution.py:64
  125.8 2.3 %copy.69 = bf16[1,2048,256]{2,1,0:T(8,128)(2,1)} copy(bf16[1,2048,256]{1,2,0:T(8,128)(2,1)} %bitcast.113) | data formatting | bytes 2097152 | tf_op jit(solution)/shard_map/stack;reshape | solution.py:85
  128.0 9.2 %fusion.20 = bf16[2,2048,128]{1,2,0:T(8,128)(2,1)S(1)} fusion(bf16[2,8,256,2048]{2,3,1,0:T(8,128)(2,1)} %fusion.1, bf16[256,2,8,128]{0,3,2,1:T(8,128)(2,1)S(1)} %bitcast.104), kind=kOutput, calls=%fused_computation.21 | convolution fusion | flops 2148532224 | bytes 18874368 | tf_op jit(solution)/shard_map/kgrn,rkgd->nkd/dot_general | solution.py:79
  137.2 0.5 copy.68
  137.8 2.8 %pad_maximum_fusion = bf16[2,2048,256]{2,1,0:T(8,128)(2,1)} fusion(bf16[1,2048,256]{2,1,0:T(8,128)(2,1)} %copy.69, bf16[1,2048,256]{2,1,0:T(8,128)(2,1)S(1)} %copy.68), kind=kLoop, calls=%fused_computation.23 | loop fusion | flops 1048576 | bytes 4194304 | tf_op jit(solution)/shard_map/stack | solution.py:85
  140.5 0.0 reduce-scatter.2.cloned.1.call-update
  140.6 10.3 %fusion.26 = bf16[256,2,8,128]{3,0,2,1:T(8,128)(2,1)S(1)} fusion(bf16[2,8,256,2048]{2,3,1,0:T(8,128)(2,1)} %fusion.1, bf16[2048,2,128,1]{0,2,3,1:T(8,128)(2,1)S(1)} %bitcast.106), kind=kOutput, calls=%fused_computation.30 | convolution fusion | flops 2148532224 | bytes 18874368 | tf_op jit(solution)/shard_map/kgrn,nkd->rkgd/dot_general | solution.py:72
  150.9 0.7 copy.62
  151.6 0.5 convert_element_type.42
  152.1 27.7 %all_to_all.32 = bf16[4,64,2048]{2,1,0:T(8,128)(2,1)S(1)} all-to-all(bf16[4,64,2048]{2,1,0:T(8,128)(2,1)S(1)} %convert_element_type.42), channel_id=1, replica_groups=mesh['dp'=8,'tensor'=4] {'tensor'}, dimensions={0} | all-to-all | bytes 2097152 | tf_op jit(solution)/shard_map/all_to_all | solution.py:131
  179.8 1.0 copy.88
  180.8 0.2 reduce-scatter.2.cloned.1.call-done
  (4 shorter events, 0.0 us)
Async XLA Ops:
  7.2 39.8 %all-gather.2.cloned.1.call-start = ((), (), s32[]{:S(2)}) async-start(), calls=%async_computation.3 | async-start | bytes 2359296 | tf_op jit(solution)/shard_map/all_gather | solution.py:118
  11.3 32.0 %all-to-all-start = ((bf16[64,4,2048]{2,0,1:T(8,128)(2,1)}), bf16[64,4,2048]{2,0,1:T(8,128)(2,1)S(1)}, u32[]{:S(2)}, u32[]{:S(2)}) async-start(bf16[64,4,2048]{2,0,1:T(8,128)(2,1)} %bitcast.102), calls=%async_computation | async-start | bytes 2097152 | tf_op jit(solution)/shard_map/all_to_all | solution.py:30
  17.6 163.4 %reduce-scatter.2.cloned.1.call-start = ((), (), s32[]{:S(2)}) async-start(), calls=%async_computation.4 | async-start | bytes 2359296 | tf_op jit(solution)/shard_map/reduce_scatter | solution.py:129
  48.7 27.9 %copy-start.1 = (bf16[1,2048,256]{1,2,0:T(8,128)(2,1)}, bf16[1,2048,256]{1,2,0:T(8,128)(2,1)S(1)}, u32[]{:S(2)}) copy-start(bf16[1,2048,256]{1,2,0:T(8,128)(2,1)S(1)} %get-tuple-element.2) | copy-start | bytes 3145732
  48.7 27.9 %copy-start = (bf16[256,2,8,128]{0,3,2,1:T(8,128)(2,1)S(1)}, bf16[256,2,8,128]{0,3,2,1:T(8,128)(2,1)}, u32[]{:S(2)}) copy-start(bf16[256,2,8,128]{0,3,2,1:T(8,128)(2,1)} %copy.58) | copy-start | bytes 3145732
Sparse Core Ops, SparseCore 0:
  10.4 30.8 all-gather.1
  140.7 40.2 reduce-scatter.1
where the time goes:
time: 188 us
  matrix products  82.2 us (44%)
  blocking collectives  27.7 us (15%)
  waiting for transfers between devices  22.8 us (12%)
  other arithmetic  18.9 us (10%)
  local copies, waits for them, and re-layouts  15.9 us (8%)
  between operations  14.2 us (8%)
  starting transfers between devices  6.36 us (3%)
    all_to_all x1, blocking collectives, body(): lax.all_to_all(query_low, 'tensor', split_axis=0, concat_axis=1, tiled=True)  27.7 us
    all_to_all x1, waiting for transfers between devices, body(): lax.all_to_all(grad_out, 'tensor', split_axis=1, concat_axis=0, tiled=True)  22.5 us
    dot_general x1, matrix products, backward_parts(): jnp.einsum('rkgd,nkd->kgrn', g_four, values_three, preferred_element_type...  19.8 us
    dot_general x1, matrix products, key_term(): jnp.einsum('kgrn,rkgd->nkd', attend_low, g_four, preferred_element_type=j...  15.4 us
    reduce_sum x1, other arithmetic, compute(): return (new_top, jnp.sum(weights, axis=-1), added)  14.4 us
    dot_general x1, matrix products, compute(): jnp.einsum('kgrn,nkd->kgrd', weights.astype(jnp.bfloat16), values_three,...  13.9 us
    dot_general x1, matrix products, logits_of(): jnp.einsum('rkgd,nkd->kgrn', q_four, keys_three, preferred_element_type=j...  13.5 us
    dot_general x1, matrix products, query_term(): jnp.einsum('kgrn,nkd->rkgd', slopes, keys_three, preferred_element_type=j...  10.3 us
  transfers between devices with their start and end apart: 3, of which 2 were waited for; matrix products, arithmetic and copies ran while one was open for 12% of the time, Pallas kernels for 0%

commit v1 on v0

v1 whole, which is shorter than its diff:
```python
import functools
import math

import jax
import jax.numpy as jnp
from jax import lax
from jax.experimental import pallas as pl
from jax.experimental.pallas import tpu as pltpu
from jax.sharding import PartitionSpec as P

HEAD_DIM = 128
GROUP = 8
PAIR = 2
MESH = pl.DeviceIdType.MESH
INV_ROOT = 1.0 / math.sqrt(HEAD_DIM)
EXP_SCALE = INV_ROOT * math.log2(math.e)


def dot(a, b):
    return jnp.dot(a, b, preferred_element_type=jnp.float32)


def dot_t(a, b):
    return lax.dot_general(a, b, (((1,), (1,)), ((), ())), preferred_element_type=jnp.float32)


def kernel(
    n_dp, n_t, back, len_ref, q_hbm, kv_hbm, go_hbm, gq_hbm, gkv_ref,
    q, g, dq, win, key_t, bias, prob, push, slope, acc, stage, own, recv,
    q_sem, kv_own_sem, g_own_sem, dq_own_sem,
    g_send, g_recv, kv_send, kv_recv, dq_send, dq_recv, dkv_send, dkv_recv,
):
    d = lax.axis_index("dp")
    t = lax.axis_index("tensor")
    rows, width = q.shape
    kv_heads = win.shape[0]
    blocks = back + 1
    slice_rows = go_hbm.shape[0]
    chunk_width = PAIR * HEAD_DIM
    chunks = width // chunk_width
    chunks_per_kv = GROUP // PAIR

    barrier = pltpu.get_barrier_semaphore()
    for step in range(1, n_dp):
        pl.semaphore_signal(barrier, inc=1, device_id=(lax.rem(d + step, n_dp), t), device_id_type=MESH)
    for step in range(1, n_t):
        pl.semaphore_signal(barrier, inc=1, device_id=(d, lax.rem(t + step, n_t)), device_id_type=MESH)

    def key_block(b):
        return pl.ds(b * rows, rows)

    q_copy = pltpu.make_async_copy(q_hbm, q, q_sem)
    q_copy.start()

    def kv_own_copy(c):
        return pltpu.make_async_copy(
            kv_hbm.at[:, :, pl.ds(c * HEAD_DIM, HEAD_DIM)],
            win.at[c, :, key_block(back), :],
            kv_own_sem.at[c],
        )

    for c in range(kv_heads):
        kv_own_copy(c).start()
    own_columns = pl.ds(pl.multiple_of(t * width, width), width)
    own_rows = pl.ds(pl.multiple_of(t * slice_rows, slice_rows), slice_rows)
    g_own_copy = pltpu.make_async_copy(go_hbm.at[:, own_columns], g.at[own_rows, :], g_own_sem)
    g_own_copy.start()

    pl.semaphore_wait(barrier, n_dp - 1 + n_t - 1)

    def kv_copy(c, step):
        return pltpu.make_async_remote_copy(
            src_ref=kv_hbm.at[:, :, pl.ds(c * HEAD_DIM, HEAD_DIM)],
            dst_ref=win.at[c, :, key_block(back - step), :],
            send_sem=kv_send.at[c, step - 1],
            recv_sem=kv_recv.at[c, step - 1],
            device_id=(lax.rem(d + step, n_dp), t),
            device_id_type=MESH,
        )

    def columns_of(holder, chunk):
        return pl.ds(pl.multiple_of(holder * width + chunk * chunk_width, chunk_width), chunk_width)

    def g_copy(chunk, step):
        target = lax.rem(t + step, n_t)
        return pltpu.make_async_remote_copy(
            src_ref=go_hbm.at[:, columns_of(target, chunk)],
            dst_ref=g.at[own_rows, columns_of(0, chunk)],
            send_sem=g_send.at[chunk, step - 1],
            recv_sem=g_recv.at[chunk, step - 1],
            device_id=(d, target),
            device_id_type=MESH,
        )

    def dq_copy(chunk, step):
        target = lax.rem(t + step, n_t)
        return pltpu.make_async_remote_copy(
            src_ref=dq.at[pl.ds(pl.multiple_of(target * slice_rows, slice_rows), slice_rows), columns_of(0, chunk)],
            dst_ref=gq_hbm.at[:, columns_of(t, chunk)],
            send_sem=dq_send.at[chunk, step - 1],
            recv_sem=dq_recv.at[chunk, step - 1],
            device_id=(d, target),
            device_id_type=MESH,
        )

    def dq_own_copy(chunk):
        return pltpu.make_async_copy(
            dq.at[own_rows, columns_of(0, chunk)], gq_hbm.at[:, columns_of(t, chunk)], dq_own_sem.at[chunk]
        )

    def dkv_copy(c, step):
        return pltpu.make_async_remote_copy(
            src_ref=stage.at[c, :, key_block(back - step), :],
            dst_ref=recv.at[c, step - 1],
            send_sem=dkv_send.at[c, step - 1],
            recv_sem=dkv_recv.at[c, step - 1],
            device_id=(lax.rem(d + n_dp - step, n_dp), t),
            device_id_type=MESH,
        )

    def send_kv(c):
        for step in range(1, blocks):
            @pl.when(d + step < n_dp)
            def _(step=step):
                kv_copy(c, step).start()

    send_kv(0)

    def send_g(chunk, carry):
        for step in range(1, n_t):
            g_copy(chunk, step).start()
        return carry

    lax.fori_loop(0, chunks, send_g, 0)
    for c in range(1, kv_heads):
        send_kv(c)

    for step in range(1, blocks):
        @pl.when(d < step)
        def _(step=step):
            win[:, :, key_block(back - step), :] = jnp.zeros((kv_heads, 2, rows, HEAD_DIM), jnp.bfloat16)

    pieces = len_ref.shape[0]
    ends = []
    total = jnp.int32(0)
    for piece in range(pieces):
        total = total + len_ref[piece]
        ends.append(total)
    query_ids = d * rows + lax.broadcasted_iota(jnp.int32, (8, rows), 1)
    query_piece = jnp.zeros((8, rows), jnp.int32)
    query_prompt = jnp.zeros((8, rows), jnp.int32)
    for piece in range(pieces):
        past = (query_ids >= ends[piece]).astype(jnp.int32)
        query_piece = query_piece + past
        if piece % 3 == 2:
            query_prompt = query_prompt + 3 * past
    query_ids, query_piece, query_prompt = query_ids[:1], query_piece[:1], query_prompt[:1]

    def mask_block(b, carry):
        key_ids = (d - back + b) * rows + lax.broadcasted_iota(jnp.int32, (rows, rows), 0)
        key_piece = jnp.zeros((rows, rows), jnp.int32)
        for piece in range(pieces):
            key_piece = key_piece + (key_ids >= ends[piece]).astype(jnp.int32)
        allowed = (key_ids <= query_ids) & (key_ids >= 0) & (
            (key_piece == query_piece) | (key_piece == query_prompt)
        )
        bias[pl.ds(pl.multiple_of(b * rows, rows), rows), :] = jnp.where(allowed, jnp.float32(0.0), jnp.float32(-1e30))
        return carry

    lax.fori_loop(0, blocks, mask_block, 0)
    q_copy.wait()
    g_own_copy.wait()

    def one_chunk(chunk, carry):
        c = chunk // chunks_per_kv
        place = lax.rem(chunk, chunks_per_kv)

        @pl.when(place == 0)
        def _():
            pltpu.make_async_copy(
                kv_hbm.at[:, :, pl.ds(0, HEAD_DIM)], win.at[c, :, key_block(back), :], kv_own_sem.at[c]
            ).wait()
            for step in range(1, blocks):
                @pl.when(d >= step)
                def _(step=step):
                    pltpu.make_async_remote_copy(
                        src_ref=kv_hbm.at[:, :, pl.ds(0, HEAD_DIM)],
                        dst_ref=win.at[c, :, key_block(back - step), :],
                        send_sem=kv_send.at[c, step - 1],
                        recv_sem=kv_recv.at[c, step - 1],
                        device_id=(lax.rem(d + step, n_dp), t),
                        device_id_type=MESH,
                    ).wait_recv()
            for b in range(blocks):
                key_t[:, key_block(b)] = win[c, 0, key_block(b), :].T
            acc[...] = jnp.zeros_like(acc)

        for step in range(1, n_t):
            g_copy(chunk, step).wait_recv()

        def heads_of(ref):
            return jnp.concatenate(
                [
                    ref[:, pl.ds(pl.multiple_of(chunk * chunk_width + u * HEAD_DIM, HEAD_DIM), HEAD_DIM)]
                    for u in range(PAIR)
                ],
                axis=0,
            )

        q_rows = heads_of(q)
        g_rows = heads_of(g)
        top = None
        for b in range(blocks):
            scores = dot_t(win[c, 0, key_block(b), :], q_rows)
            scores = scores + jnp.concatenate([bias[key_block(b), :]] * PAIR, axis=1)
            prob[key_block(b), :] = scores
            block_top = jnp.max(scores, axis=0, keepdims=True)
            top = block_top if top is None else jnp.maximum(top, block_top)
        weight_sum = jnp.zeros_like(top)
        push_sum = jnp.zeros_like(top)
        for b in range(blocks):
            weights = jnp.exp2((prob[key_block(b), :] - top) * EXP_SCALE)
            pushed = dot_t(win[c, 1, key_block(b), :], g_rows)
            prob[key_block(b), :] = weights
            push[key_block(b), :] = pushed
            weight_sum = weight_sum + jnp.sum(weights, axis=0, keepdims=True)
            push_sum = push_sum + jnp.sum(weights * pushed, axis=0, keepdims=True)
        inverse = 1.0 / weight_sum
        delta = push_sum * inverse
        for b in range(blocks):
            attend = prob[key_block(b), :] * inverse
            slopes = (attend * (push[key_block(b), :] - delta)).astype(jnp.bfloat16)
            slope[key_block(b), :] = slopes
            acc[0, key_block(b), :] += dot(slopes, q_rows)
            acc[1, key_block(b), :] += dot(attend.astype(jnp.bfloat16), g_rows)
        query_grad = dot(key_t[...], slope[...]) * INV_ROOT
        for u in range(PAIR):
            dq[:, pl.ds(pl.multiple_of(chunk * chunk_width + u * HEAD_DIM, HEAD_DIM), HEAD_DIM)] = (
                query_grad[:, u * rows : (u + 1) * rows].T.astype(jnp.bfloat16)
            )
        for step in range(1, n_t):
            dq_copy(chunk, step).start()
        dq_own_copy(chunk).start()

        @pl.when(place == chunks_per_kv - 1)
        def _():
            for b in range(blocks):
                key_part = acc[0, key_block(b), :] * INV_ROOT
                value_part = acc[1, key_block(b), :]
                if b == back:
                    own[c, 0] = key_part
                    own[c, 1] = value_part
                else:
                    stage[c, 0, key_block(b), :] = key_part.astype(jnp.bfloat16)
                    stage[c, 1, key_block(b), :] = value_part.astype(jnp.bfloat16)
            for step in range(1, blocks):
                @pl.when(d >= step)
                def _(step=step):
                    dkv_copy(c, step).start()

        return carry

    lax.fori_loop(0, chunks, one_chunk, 0)

    for c in range(kv_heads):
        for step in range(1, blocks):
            @pl.when(d + step < n_dp)
            def _(c=c, step=step):
                kv_copy(c, step).wait_send()
                dkv_copy(c, step).wait_recv()
                own[c] += recv[c, step - 1].astype(jnp.float32)
        gkv_ref[:, :, c * HEAD_DIM : (c + 1) * HEAD_DIM] = own[c].astype(jnp.bfloat16)
    for c in range(kv_heads):
        for step in range(1, blocks):
            @pl.when(d >= step)
            def _(c=c, step=step):
                dkv_copy(c, step).wait_send()

    def finish(chunk, carry):
        for step in range(1, n_t):
            g_copy(chunk, step).wait_send()
            dq_copy(chunk, step).wait()
        dq_own_copy(chunk).wait()
        return carry

    lax.fori_loop(0, chunks, finish, 0)


def body(n_dp, n_t, queries, keys_values, grad_out, piece_lengths):
    rows, width = queries.shape
    kv_heads = keys_values.shape[2] // HEAD_DIM
    tokens = rows * n_dp
    group_rows = 36 * (tokens // 64)
    back = min(n_dp - 1, -(-(group_rows - 1) // rows))
    keys = (back + 1) * rows
    chunks = width // (PAIR * HEAD_DIM)
    bf16, f32 = jnp.bfloat16, jnp.float32
    dma = pltpu.SemaphoreType.DMA
    lanes = PAIR * rows
    flops = 5 * 2 * rows * keys * width
    return pl.pallas_call(
        functools.partial(kernel, n_dp, n_t, back),
        out_shape=(
            jax.ShapeDtypeStruct(grad_out.shape, bf16),
            jax.ShapeDtypeStruct(keys_values.shape, bf16),
        ),
        in_specs=[
            pl.BlockSpec(memory_space=pltpu.SMEM),
            pl.BlockSpec(memory_space=pl.ANY),
            pl.BlockSpec(memory_space=pl.ANY),
            pl.BlockSpec(memory_space=pl.ANY),
        ],
        out_specs=(pl.BlockSpec(memory_space=pl.ANY), pl.BlockSpec(memory_space=pltpu.VMEM)),
        scratch_shapes=[
            pltpu.VMEM((rows, width), bf16),
            pltpu.VMEM((rows, width), bf16),
            pltpu.VMEM((rows, width), bf16),
            pltpu.VMEM((kv_heads, 2, keys, HEAD_DIM), bf16),
            pltpu.VMEM((HEAD_DIM, keys), bf16),
            pltpu.VMEM((keys, rows), f32),
            pltpu.VMEM((keys, lanes), f32),
            pltpu.VMEM((keys, lanes), f32),
            pltpu.VMEM((keys, lanes), bf16),
            pltpu.VMEM((2, keys, HEAD_DIM), f32),
            pltpu.VMEM((kv_heads, 2, keys, HEAD_DIM), bf16),
            pltpu.VMEM((kv_heads, 2, rows, HEAD_DIM), f32),
            pltpu.VMEM((kv_heads, back, 2, rows, HEAD_DIM), bf16),
            dma(()),
            dma((kv_heads,)),
            dma(()),
            dma((chunks,)),
            dma((chunks, n_t - 1)),
            dma((chunks, n_t - 1)),
            dma((kv_heads, back)),
            dma((kv_heads, back)),
            dma((chunks, n_t - 1)),
            dma((chunks, n_t - 1)),
            dma((kv_heads, back)),
            dma((kv_heads, back)),
        ],
        compiler_params=pltpu.CompilerParams(
            collective_id=0, has_side_effects=True, vmem_limit_bytes=56 * 1024 * 1024
        ),
        cost_estimate=pl.CostEstimate(flops=flops, bytes_accessed=8 * rows * width, transcendentals=0),
    )(piece_lengths, queries, keys_values, grad_out)


def solution(mesh):
    return jax.shard_map(
        functools.partial(body, mesh.shape["dp"], mesh.shape["tensor"]),
        mesh=mesh,
        in_specs=(P("dp", "tensor"), P(None, "dp", "tensor"), P(("dp", "tensor"), None), P()),
        out_specs=(P(("dp", "tensor"), None), P(None, "dp", "tensor")),
        check_vma=False,
    )
```

time: 188 us -> 64.3 us (0.34)
  matrix products: 82.2 us -> 0 us
  Pallas kernels: 0 us -> 60.5 us
  blocking collectives: 27.7 us -> 0 us
  waiting for transfers between devices: 22.8 us -> 0 us
  other arithmetic: 18.9 us -> 0 us
  between operations: 14.2 us -> 0.65 us
  local copies, waits for them, and re-layouts: 15.9 us -> 3.01 us
  starting transfers between devices: 6.36 us -> 0 us
    dot_general x6 -> x0, matrix products: 82.2 us -> none  [the longest x1 19.8 us: backward_parts(): jnp.einsum('rkgd,nkd->kgrn', g_four, values_three, preferred_element_type...]
    pallas_call x0 -> x1, Pallas kernels: none -> 60.5 us  [body(): pl.pallas_call(functools.partial(kernel, n_dp, n_t, back), out_shape=(jax...]
    all_to_all x1 -> x0, blocking collectives: 27.7 us -> none  [body(): lax.all_to_all(query_low, 'tensor', split_axis=0, concat_axis=1, tiled=True)]
    all_to_all x1 -> x0, waiting for transfers between devices: 22.5 us -> none  [body(): lax.all_to_all(grad_out, 'tensor', split_axis=1, concat_axis=0, tiled=True)]
    reduce_sum x3 -> x0, other arithmetic: 14.5 us -> none  [the longest x1 14.4 us: compute(): return (new_top, jnp.sum(weights, axis=-1), added)]
    all_to_all x1 -> x0, starting transfers between devices: 6.32 us -> none  [body(): lax.all_to_all(grad_out, 'tensor', split_axis=1, concat_axis=0, tiled=True)]
    reshape x2 -> x0, local copies, waits for them, and re-layouts: 3.89 us -> none  [the longest x1 2.42 us: body(): g_four = grad_local.reshape(row_count, kv_dev, group_size, head_dim)]
    another operation x3 -> x0, other arithmetic: 3.61 us -> none  [the longest x1 2.77 us: key_term(): jnp.stack([key_part.reshape(key_count, kv_width), value_part.reshape(key_...]
  transfers between devices with their start and end apart: 3 -> 0, of which waited for: 2 -> 0; matrix products, arithmetic and copies ran while one was open for 12% -> 0% of each run, Pallas kernels for 0% -> 0%
where the time goes in v1:
time: 64.3 us; the launch traced here: 64.1 us
  Pallas kernels  60.5 us (94%)
  local copies, waits for them, and re-layouts  3.01 us (5%)
  between operations  0.65 us (1%)
    pallas_call x1, Pallas kernels, body(): pl.pallas_call(functools.partial(kernel, n_dp, n_t, back), out_shape=(jax...  60.5 us
    unnamed x4, local copies, waits for them, and re-layouts  3.01 us

profile of v1, /device:TPU:0, one launch (start us, length us, event | category | flops | bytes accessed | tf_op | source)
XLA Modules:
  0.0 64.1 jit_solution(8294103213971223082)
XLA Ops:
  0.6 60.5 %shard_map.59 = (bf16[64,8192]{1,0:T(8,128)(2,1)}, bf16[2,256,256]{2,1,0:T(8,128)(2,1)}) custom-call(s32[12]{0:T(128)} %len_ref.1, bf16[256,2048]{1,0:T(8,128)(2,1)} %q_hbm.1, bf16[2,256,256]{2,1,0:T(8,128)(2,1)} %kv_hbm.1, bf16[64,8192]{1,0:T(8,128)(2,1)} %go_hbm.1), custom_call_target="tpu_custom_call" | custom-call | flops 8053063680 | bytes 4194304 | tf_op jit(solution)/shard_map/pallas_call | solution.py:301
  61.1 0.0 copy-start
  61.1 2.3 %copy.8 = bf16[64,8192]{1,0:T(8,128)(2,1)} copy(bf16[64,8192]{1,0:T(8,128)(2,1)} %get-tuple-element.4) | data formatting | bytes 2097152
  63.4 0.0 copy-done
  63.4 0.7 %copy.9 = bf16[2,256,256]{2,1,0:T(8,128)(2,1)} copy(bf16[2,256,256]{2,1,0:T(8,128)(2,1)S(1)} %copy-done) | data formatting | bytes 524288
Async XLA Ops:
  61.1 2.3 %copy-start = (bf16[2,256,256]{2,1,0:T(8,128)(2,1)S(1)}, bf16[2,256,256]{2,1,0:T(8,128)(2,1)}, u32[]{:S(2)}) copy-start(bf16[2,256,256]{2,1,0:T(8,128)(2,1)} %get-tuple-element.5) | copy-start | bytes 786436

commit v2 on v1

--- a/solution.py
+++ b/solution.py
@@ -26,15 +26,30 @@
 
 def kernel(
     n_dp, n_t, back, len_ref, q_hbm, kv_hbm, go_hbm, gq_hbm, gkv_ref,
-    q, g, dq, win, key_t, bias, prob, push, slope, acc, stage, own, recv,
+    q, g, dq, win, key_t, bias, prob, push, slope, acc, stage, own, recv, swap,
     q_sem, kv_own_sem, g_own_sem, dq_own_sem,
     g_send, g_recv, kv_send, kv_recv, dq_send, dq_recv, dkv_send, dkv_recv,
+    pass_send, pass_recv, swap_send, swap_recv,
 ):
     d = lax.axis_index("dp")
     t = lax.axis_index("tensor")
     rows, width = q.shape
     kv_heads = win.shape[0]
     blocks = back + 1
+    core = lax.rem(d, 2)
+    partner = d + 1 - 2 * core
+    full = (back - 1) // 2
+    hops = [(j, 2 * j + 2) for j in range(full)] + [(full, 1), (full + 1, back)]
+
+    def has_later(step):
+        if step == 1:
+            return core == 0
+        return (d + step < n_dp) & ((core == 1) | (step % 2 == 0))
+
+    def has_earlier(step):
+        if step == 1:
+            return core == 1
+        return (d >= step) & ((core == 0) | (step % 2 == 0))
     slice_rows = go_hbm.shape[0]
     chunk_width = PAIR * HEAD_DIM
     chunks = width // chunk_width
@@ -68,15 +83,78 @@
 
     pl.semaphore_wait(barrier, n_dp - 1 + n_t - 1)
 
-    def kv_copy(c, step):
+    def dynamic_block(b):
+        return pl.ds(pl.multiple_of(b * rows, rows), rows)
+
+    def kv_copy(c, slot, step):
         return pltpu.make_async_remote_copy(
             src_ref=kv_hbm.at[:, :, pl.ds(c * HEAD_DIM, HEAD_DIM)],
             dst_ref=win.at[c, :, key_block(back - step), :],
-            send_sem=kv_send.at[c, step - 1],
-            recv_sem=kv_recv.at[c, step - 1],
+            send_sem=kv_send.at[c, slot],
+            recv_sem=kv_recv.at[c, slot],
             device_id=(lax.rem(d + step, n_dp), t),
             device_id_type=MESH,
         )
+
+    def pass_copy(c, j):
+        step = 2 * j + 2
+        return pltpu.make_async_remote_copy(
+            src_ref=win.at[c, :, key_block(back - step), :],
+            dst_ref=win.at[c, :, dynamic_block(back - step - 1 + 2 * core), :],
+            send_sem=pass_send.at[c, j],
+            recv_sem=pass_recv.at[c, j],
+            device_id=(partner, t),
+            device_id_type=MESH,
+        )
+
+    def pass_arrival(c, j):
+        step = 2 * j + 2
+        return pltpu.make_async_remote_copy(
+            src_ref=win.at[c, :, key_block(back - step), :],
+            dst_ref=win.at[c, :, dynamic_block(back - step + 1 - 2 * core), :],
+            send_sem=pass_send.at[c, j],
+            recv_sem=pass_recv.at[c, j],
+            device_id=(partner, t),
+            device_id_type=MESH,
+        )
+
+    def pass_on(c):
+        for j in range(full):
+            @pl.when(has_earlier(2 * j + 2))
+            def _(j=j):
+                kv_copy(c, j, 2 * j + 2).wait_recv()
+                pass_copy(c, j).start()
+
+    def swap_copy(c, j):
+        return pltpu.make_async_remote_copy(
+            src_ref=stage.at[c, :, dynamic_block(back - 2 * j - 1 - 2 * core), :],
+            dst_ref=swap.at[c, j],
+            send_sem=swap_send.at[c, j],
+            recv_sem=swap_recv.at[c, j],
+            device_id=(partner, t),
+            device_id_type=MESH,
+        )
+
+    def dkv_copy(c, slot, step):
+        return pltpu.make_async_remote_copy(
+            src_ref=stage.at[c, :, key_block(back - step), :],
+            dst_ref=recv.at[c, slot],
+            send_sem=dkv_send.at[c, slot],
+            recv_sem=dkv_recv.at[c, slot],
+            device_id=(lax.rem(d + n_dp - step, n_dp), t),
+            device_id_type=MESH,
+        )
+
+    def send_sums(c):
+        for j in range(full):
+            @pl.when(has_earlier(2 * j + 2))
+            def _(j=j):
+                step = 2 * j + 2
+                swap_copy(c, j).wait_recv()
+                stage[c, :, key_block(back - step), :] = (
+                    stage[c, :, key_block(back - step), :].astype(jnp.float32) + swap[c, j].astype(jnp.float32)
+                ).astype(jnp.bfloat16)
+                dkv_copy(c, j, step).start()
 
     def columns_of(holder, chunk):
         return pl.ds(pl.multiple_of(holder * width + chunk * chunk_width, chunk_width), chunk_width)
@@ -108,21 +186,11 @@
             dq.at[own_rows, columns_of(0, chunk)], gq_hbm.at[:, columns_of(t, chunk)], dq_own_sem.at[chunk]
         )
 
-    def dkv_copy(c, step):
-        return pltpu.make_async_remote_copy(
-            src_ref=stage.at[c, :, key_block(back - step), :],
-            dst_ref=recv.at[c, step - 1],
-            send_sem=dkv_send.at[c, step - 1],
-            recv_sem=dkv_recv.at[c, step - 1],
-            device_id=(lax.rem(d + n_dp - step, n_dp), t),
-            device_id_type=MESH,
-        )
-
     def send_kv(c):
-        for step in range(1, blocks):
-            @pl.when(d + step < n_dp)
-            def _(step=step):
-                kv_copy(c, step).start()
+        for slot, step in hops:
+            @pl.when(has_later(step))
+            def _(slot=slot, step=step):
+                kv_copy(c, slot, step).start()
 
     send_kv(0)
 
@@ -170,6 +238,7 @@
     lax.fori_loop(0, blocks, mask_block, 0)
     q_copy.wait()
     g_own_copy.wait()
+    pass_on(0)
 
     def one_chunk(chunk, carry):
         c = chunk // chunks_per_kv
@@ -180,17 +249,21 @@
             pltpu.make_async_copy(
                 kv_hbm.at[:, :, pl.ds(0, HEAD_DIM)], win.at[c, :, key_block(back), :], kv_own_sem.at[c]
             ).wait()
-            for step in range(1, blocks):
-                @pl.when(d >= step)
-                def _(step=step):
+            for slot, step in hops[full:]:
+                @pl.when(has_earlier(step))
+                def _(slot=slot, step=step):
                     pltpu.make_async_remote_copy(
                         src_ref=kv_hbm.at[:, :, pl.ds(0, HEAD_DIM)],
                         dst_ref=win.at[c, :, key_block(back - step), :],
-                        send_sem=kv_send.at[c, step - 1],
-                        recv_sem=kv_recv.at[c, step - 1],
+                        send_sem=kv_send.at[c, slot],
+                        recv_sem=kv_recv.at[c, slot],
                         device_id=(lax.rem(d + step, n_dp), t),
                         device_id_type=MESH,
                     ).wait_recv()
+            for j in range(full):
+                @pl.when(has_earlier(2 * j + 2))
+                def _(j=j):
+                    pass_arrival(c, j).wait_recv()
             for b in range(blocks):
                 key_t[:, key_block(b)] = win[c, 0, key_block(b), :].T
             acc[...] = jnp.zeros_like(acc)
@@ -253,28 +326,47 @@
                 else:
                     stage[c, 0, key_block(b), :] = key_part.astype(jnp.bfloat16)
                     stage[c, 1, key_block(b), :] = value_part.astype(jnp.bfloat16)
-            for step in range(1, blocks):
-                @pl.when(d >= step)
-                def _(step=step):
-                    dkv_copy(c, step).start()
+            for j in range(full):
+                @pl.when(has_earlier(2 * j + 2))
+                def _(j=j):
+                    swap_copy(c, j).start()
+            for slot, step in hops[full:]:
+                @pl.when(has_earlier(step))
+                def _(slot=slot, step=step):
+                    dkv_copy(c, slot, step).start()
+
+        for later in range(1, kv_heads):
+            @pl.when(chunk == (later - 1) * chunks_per_kv + 1)
+            def _(later=later):
+                pass_on(later)
+
+            @pl.when(chunk == later * chunks_per_kv)
+            def _(later=later):
+                send_sums(later - 1)
 
         return carry
 
     lax.fori_loop(0, chunks, one_chunk, 0)
+    send_sums(kv_heads - 1)
 
     for c in range(kv_heads):
-        for step in range(1, blocks):
-            @pl.when(d + step < n_dp)
-            def _(c=c, step=step):
-                kv_copy(c, step).wait_send()
-                dkv_copy(c, step).wait_recv()
-                own[c] += recv[c, step - 1].astype(jnp.float32)
+        for slot, step in hops:
+            @pl.when(has_later(step))
+            def _(c=c, slot=slot, step=step):
+                kv_copy(c, slot, step).wait_send()
+                dkv_copy(c, slot, step).wait_recv()
+                own[c] += recv[c, slot].astype(jnp.float32)
         gkv_ref[:, :, c * HEAD_DIM : (c + 1) * HEAD_DIM] = own[c].astype(jnp.bfloat16)
     for c in range(kv_heads):
-        for step in range(1, blocks):
-            @pl.when(d >= step)
-            def _(c=c, step=step):
-                dkv_copy(c, step).wait_send()
+        for slot, step in hops:
+            @pl.when(has_earlier(step))
+            def _(c=c, slot=slot, step=step):
+                dkv_copy(c, slot, step).wait_send()
+        for j in range(full):
+            @pl.when(has_earlier(2 * j + 2))
+            def _(c=c, j=j):
+                pass_copy(c, j).wait_send()
+                swap_copy(c, j).wait_send()
 
     def finish(chunk, carry):
         for step in range(1, n_t):
@@ -286,19 +378,48 @@
     lax.fori_loop(0, chunks, finish, 0)
 
 
+def hand_over(query_grad, key_grad):
+    slice_rows, width = query_grad.shape
+    slabs = slice_rows // 16
+    halves = 2
+
+    def move(a, b, a_out, b_out, sems):
+        copies = [pltpu.make_async_copy(b, b_out, sems.at[slabs * halves])]
+        for i in range(slabs):
+            for half in range(halves):
+                part = (pl.ds(i * 16, 16), pl.ds(half * (width // halves), width // halves))
+                copies.append(pltpu.make_async_copy(a.at[part], a_out.at[part], sems.at[i * halves + half]))
+        for copy in copies:
+            copy.start()
+        for copy in copies:
+            copy.wait()
+
+    return pl.pallas_call(
+        move,
+        out_shape=(
+            jax.ShapeDtypeStruct(query_grad.shape, query_grad.dtype),
+            jax.ShapeDtypeStruct(key_grad.shape, key_grad.dtype),
+        ),
+        in_specs=[pl.BlockSpec(memory_space=pl.ANY)] * 2,
+        out_specs=(pl.BlockSpec(memory_space=pl.ANY), pl.BlockSpec(memory_space=pl.ANY)),
+        scratch_shapes=[pltpu.SemaphoreType.DMA((slabs * halves + 1,))],
+    )(query_grad, key_grad)
+
+
 def body(n_dp, n_t, queries, keys_values, grad_out, piece_lengths):
     rows, width = queries.shape
     kv_heads = keys_values.shape[2] // HEAD_DIM
     tokens = rows * n_dp
     group_rows = 36 * (tokens // 64)
-    back = min(n_dp - 1, -(-(group_rows - 1) // rows))
+    back = min(n_dp - 1, -(-(group_rows - 1) // rows) // 2 * 2 + 1)
+    full = (back - 1) // 2
     keys = (back + 1) * rows
     chunks = width // (PAIR * HEAD_DIM)
     bf16, f32 = jnp.bfloat16, jnp.float32
     dma = pltpu.SemaphoreType.DMA
     lanes = PAIR * rows
     flops = 5 * 2 * rows * keys * width
-    return pl.pallas_call(
+    results = pl.pallas_call(
         functools.partial(kernel, n_dp, n_t, back),
         out_shape=(
             jax.ShapeDtypeStruct(grad_out.shape, bf16),
@@ -324,25 +445,31 @@
             pltpu.VMEM((2, keys, HEAD_DIM), f32),
             pltpu.VMEM((kv_heads, 2, keys, HEAD_DIM), bf16),
             pltpu.VMEM((kv_heads, 2, rows, HEAD_DIM), f32),
-            pltpu.VMEM((kv_heads, back, 2, rows, HEAD_DIM), bf16),
+            pltpu.VMEM((kv_heads, full + 2, 2, rows, HEAD_DIM), bf16),
+            pltpu.VMEM((kv_heads, full, 2, rows, HEAD_DIM), bf16),
             dma(()),
             dma((kv_heads,)),
             dma(()),
             dma((chunks,)),
             dma((chunks, n_t - 1)),
             dma((chunks, n_t - 1)),
-            dma((kv_heads, back)),
-            dma((kv_heads, back)),
+            dma((kv_heads, full + 2)),
+            dma((kv_heads, full + 2)),
             dma((chunks, n_t - 1)),
             dma((chunks, n_t - 1)),
-            dma((kv_heads, back)),
-            dma((kv_heads, back)),
+            dma((kv_heads, full + 2)),
+            dma((kv_heads, full + 2)),
+            dma((kv_heads, full)),
+            dma((kv_heads, full)),
+            dma((kv_heads, full)),
+            dma((kv_heads, full)),
         ],
         compiler_params=pltpu.CompilerParams(
             collective_id=0, has_side_effects=True, vmem_limit_bytes=56 * 1024 * 1024
         ),
         cost_estimate=pl.CostEstimate(flops=flops, bytes_accessed=8 * rows * width, transcendentals=0),
     )(piece_lengths, queries, keys_values, grad_out)
+    return hand_over(*results)
 
 
 def solution(mesh):

time: 64.3 us -> 96.9 us (1.51)
  Pallas kernels: 60.5 us -> 96.1 us
  local copies, waits for them, and re-layouts: 3.01 us -> 0 us
    pallas_call x0 -> x1, Pallas kernels: none -> 40.9 us  [hand_over(): pl.pallas_call(move, out_shape=(jax.ShapeDtypeStruct(query_grad.shape, qu...]
    pallas_call x1, Pallas kernels: 60.5 us -> 55.2 us  [body(): pl.pallas_call(functools.partial(kernel, n_dp, n_t, back), out_shape=(jax...]
    unnamed x4 -> x0, local copies, waits for them, and re-layouts: 3.01 us -> none
where the time goes in v2:
time: 96.9 us; the launch traced here: 96.7 us
  Pallas kernels  96.1 us (99%)
    pallas_call x1, Pallas kernels, body(): pl.pallas_call(functools.partial(kernel, n_dp, n_t, back), out_shape=(jax...  55.2 us
    pallas_call x1, Pallas kernels, hand_over(): pl.pallas_call(move, out_shape=(jax.ShapeDtypeStruct(query_grad.shape, qu...  40.9 us

profile of v2, /device:TPU:0, one launch (start us, length us, event | category | flops | bytes accessed | tf_op | source)
XLA Modules:
  0.0 96.7 jit_solution(15949269408450856895)
XLA Ops:
  0.6 55.2 %shard_map.59 = (bf16[64,8192]{1,0:T(8,128)(2,1)}, bf16[2,256,256]{2,1,0:T(8,128)(2,1)}) custom-call(s32[12]{0:T(128)} %len_ref.1, bf16[256,2048]{1,0:T(8,128)(2,1)} %q_hbm.1, bf16[2,256,256]{2,1,0:T(8,128)(2,1)} %kv_hbm.1, bf16[64,8192]{1,0:T(8,128)(2,1)} %go_hbm.1), custom_call_target="tpu_custom_call" | custom-call | flops 8053063680 | bytes 4194304 | tf_op jit(solution)/shard_map/pallas_call | solution.py:422
  55.8 40.9 %shard_map.60 = (bf16[64,8192]{1,0:T(8,128)(2,1)}, bf16[2,256,256]{2,1,0:T(8,128)(2,1)}) custom-call(bf16[64,8192]{1,0:T(8,128)(2,1)} %get-tuple-element.4.a, bf16[2,256,256]{2,1,0:T(8,128)(2,1)} %get-tuple-element.5.b), custom_call_target="tpu_custom_call" | custom-call | tf_op jit(solution)/shard_map/pallas_call | solution.py:397

commit v3 on v2

--- a/solution.py
+++ b/solution.py
@@ -380,18 +380,21 @@
 
 def hand_over(query_grad, key_grad):
     slice_rows, width = query_grad.shape
-    slabs = slice_rows // 16
-    halves = 2
-
-    def move(a, b, a_out, b_out, sems):
-        copies = [pltpu.make_async_copy(b, b_out, sems.at[slabs * halves])]
-        for i in range(slabs):
-            for half in range(halves):
-                part = (pl.ds(i * 16, 16), pl.ds(half * (width // halves), width // halves))
-                copies.append(pltpu.make_async_copy(a.at[part], a_out.at[part], sems.at[i * halves + half]))
-        for copy in copies:
+    parts = 8
+
+    def move(a, b, a_out, b_out, a_held, b_held, in_sem, out_sem):
+        ways = [(b, b_held, b_out)]
+        for i in range(parts):
+            part = (slice(None), pl.ds(i * (width // parts), width // parts))
+            ways.append((a.at[part], a_held.at[part], a_out.at[part]))
+        inward = [pltpu.make_async_copy(w[0], w[1], in_sem.at[i]) for i, w in enumerate(ways)]
+        outward = [pltpu.make_async_copy(w[1], w[2], out_sem.at[i]) for i, w in enumerate(ways)]
+        for copy in inward:
             copy.start()
-        for copy in copies:
+        for first, second in zip(inward, outward):
+            first.wait()
+            second.start()
+        for copy in outward:
             copy.wait()
 
     return pl.pallas_call(
@@ -402,7 +405,13 @@
         ),
         in_specs=[pl.BlockSpec(memory_space=pl.ANY)] * 2,
         out_specs=(pl.BlockSpec(memory_space=pl.ANY), pl.BlockSpec(memory_space=pl.ANY)),
-        scratch_shapes=[pltpu.SemaphoreType.DMA((slabs * halves + 1,))],
+        scratch_shapes=[
+            pltpu.VMEM(query_grad.shape, query_grad.dtype),
+            pltpu.VMEM(key_grad.shape, key_grad.dtype),
+            pltpu.SemaphoreType.DMA((parts + 1,)),
+            pltpu.SemaphoreType.DMA((parts + 1,)),
+        ],
+        compiler_params=pltpu.CompilerParams(vmem_limit_bytes=56 * 1024 * 1024),
     )(query_grad, key_grad)
 
 

time: 96.9 us -> 58.1 us (0.60)
  Pallas kernels: 96.1 us -> 57.4 us
    pallas_call x1, Pallas kernels: 40.9 us -> 2.15 us  [hand_over(): pl.pallas_call(move, out_shape=(jax.ShapeDtypeStruct(query_grad.shape, qu...]
where the time goes in v3:
time: 58.1 us; the launch traced here: 58 us
  Pallas kernels  57.4 us (99%)
  between operations  0.64 us (1%)
    pallas_call x1, Pallas kernels, body(): pl.pallas_call(functools.partial(kernel, n_dp, n_t, back), out_shape=(jax...  55.2 us
    pallas_call x1, Pallas kernels, hand_over(): pl.pallas_call(move, out_shape=(jax.ShapeDtypeStruct(query_grad.shape, qu...  2.15 us

profile of v3, /device:TPU:0, one launch (start us, length us, event | category | flops | bytes accessed | tf_op | source)
XLA Modules:
  0.0 58.0 jit_solution(1715379964011496374)
XLA Ops:
  0.6 55.2 %shard_map.59 = (bf16[64,8192]{1,0:T(8,128)(2,1)}, bf16[2,256,256]{2,1,0:T(8,128)(2,1)}) custom-call(s32[12]{0:T(128)} %len_ref.1, bf16[256,2048]{1,0:T(8,128)(2,1)} %q_hbm.1, bf16[2,256,256]{2,1,0:T(8,128)(2,1)} %kv_hbm.1, bf16[64,8192]{1,0:T(8,128)(2,1)} %go_hbm.1), custom_call_target="tpu_custom_call" | custom-call | flops 8053063680 | bytes 4194304 | tf_op jit(solution)/shard_map/pallas_call | solution.py:431
  55.8 2.1 %shard_map.60 = (bf16[64,8192]{1,0:T(8,128)(2,1)}, bf16[2,256,256]{2,1,0:T(8,128)(2,1)}) custom-call(bf16[64,8192]{1,0:T(8,128)(2,1)} %get-tuple-element.4.a, bf16[2,256,256]{2,1,0:T(8,128)(2,1)} %get-tuple-element.5.b), custom_call_target="tpu_custom_call" | custom-call | tf_op jit(solution)/shard_map/pallas_call | solution.py:400

commit v4 on v3

--- a/solution.py
+++ b/solution.py
@@ -10,7 +10,7 @@
 
 HEAD_DIM = 128
 GROUP = 8
-PAIR = 2
+PAIR = 4
 MESH = pl.DeviceIdType.MESH
 INV_ROOT = 1.0 / math.sqrt(HEAD_DIM)
 EXP_SCALE = INV_ROOT * math.log2(math.e)

time: 58.1 us -> 57.1 us (0.983)
  Pallas kernels: 57.4 us -> 56.3 us
    pallas_call x1, Pallas kernels: 55.2 us -> 54.2 us  [body(): pl.pallas_call(functools.partial(kernel, n_dp, n_t, back), out_shape=(jax...]
where the time goes in v4:
time: 57.1 us; the launch traced here: 57 us
  Pallas kernels  56.3 us (99%)
  between operations  0.64 us (1%)
    pallas_call x1, Pallas kernels, body(): pl.pallas_call(functools.partial(kernel, n_dp, n_t, back), out_shape=(jax...  54.2 us
    pallas_call x1, Pallas kernels, hand_over(): pl.pallas_call(move, out_shape=(jax.ShapeDtypeStruct(query_grad.shape, qu...  2.15 us

profile of v4, /device:TPU:0, one launch (start us, length us, event | category | flops | bytes accessed | tf_op | source)
XLA Modules:
  0.0 57.0 jit_solution(15569248889401466705)
XLA Ops:
  0.6 54.2 %shard_map.59 = (bf16[64,8192]{1,0:T(8,128)(2,1)}, bf16[2,256,256]{2,1,0:T(8,128)(2,1)}) custom-call(s32[12]{0:T(128)} %len_ref.1, bf16[256,2048]{1,0:T(8,128)(2,1)} %q_hbm.1, bf16[2,256,256]{2,1,0:T(8,128)(2,1)} %kv_hbm.1, bf16[64,8192]{1,0:T(8,128)(2,1)} %go_hbm.1), custom_call_target="tpu_custom_call" | custom-call | flops 8053063680 | bytes 4194304 | tf_op jit(solution)/shard_map/pallas_call | solution.py:431
  54.8 2.1 %shard_map.60 = (bf16[64,8192]{1,0:T(8,128)(2,1)}, bf16[2,256,256]{2,1,0:T(8,128)(2,1)}) custom-call(bf16[64,8192]{1,0:T(8,128)(2,1)} %get-tuple-element.4.a, bf16[2,256,256]{2,1,0:T(8,128)(2,1)} %get-tuple-element.5.b), custom_call_target="tpu_custom_call" | custom-call | tf_op jit(solution)/shard_map/pallas_call | solution.py:400
